TPU v7x, 256 devices: a whole 4x4x8 slice. The times are simulated.
256 devices in a mesh: lat: 32 (over z_lo, y, x), lev: 8 (over z_hi, core).
Axes of the slice: x: 4, y: 4, z: 8 (z_hi: 4, z_lo: 2; z = z_hi * 2 + z_lo), core: 2. Of those that a mesh axis runs over, the one named last changes fastest.
Arguments:
- zonal_wind_speed: float32 [768, 64, 1152], P('lat', 'lev'), may hold values from -1 to 1
- meridional_wind_speed: float32 [768, 64, 1152], P('lat', 'lev'), may hold values from -1 to 1
- thermal_state: float32 [768, 64, 1152], P('lat', 'lev'), may hold values from 0.5 to 2
- pressure_depth: float32 [768, 64, 1152], P('lat', 'lev'), may hold values from 1 to 2
- primary_scalar_mixing: float32 [768, 64, 1152], P('lat', 'lev'), may hold values from -6 to 6
- secondary_scalar_mixing: float32 [768, 64, 1152], P('lat', 'lev'), may hold values from 0.1 to 10
- terrain_potential_height: float32 [768, 1152], P('lat'), may hold values from -6 to 6
Outputs:
- east_out: float32 [768, 64, 1152], P('lat', 'lev')
- north_out: float32 [768, 64, 1152], P('lat', 'lev')
- temperature_out: float32 [768, 64, 1152], P('lat', 'lev')
- thickness_out: float32 [768, 64, 1152], P('lat', 'lev')
- tracer_one_out: float32 [768, 64, 1152], P('lat', 'lev')
- tracer_two_out: float32 [768, 64, 1152], P('lat', 'lev')
- geopotential: float32 [768, 64, 1152], P('lat', 'lev')
All inputs are finite; a program needn't handle non-finite values.
Results may differ from a plain program's by a relative error of at most 0.00007.
Values sent between devices are 32-bit elements; how exact they have to be, the bound alone decides.
A program may use at most 128 MiB of HBM per device.

v0:
```python
import functools
import math

import jax
import jax.numpy as jnp
import numpy as np
from jax import lax
from jax.experimental import pallas as pl
from jax.experimental.pallas import tpu as pltpu
from jax.sharding import PartitionSpec as P

MESH = pl.DeviceIdType.MESH
F32 = jnp.float32
BF16 = jnp.bfloat16

ROWS, LEVS, LON = 24, 8, 1152
NLAT = 32
CHIPS = 4
LANE = 128
COURANT = 0.1
GRAD = 0.1
GAS = 0.3
TOP = 1.0
CUT = 0.5

INTERIOR = ((1, 6), (13, 5))
EDGE = len(INTERIOR)
NCHUNK = EDGE + 1


@functools.cache
def tables():
    b = np.arange(LANE)
    fwd, back = [], []
    for r in range(1, 5):
        angle = 2.0 * np.pi * ((b[:, None] * (9 * b[None, :] + r)) % LON) / LON
        mr, mi = np.cos(angle), -np.sin(angle)
        w = np.block([[mr, mi], [-mi, mr]])
        fwd.append(w)
        back.append(w.T * (2.0 / LON))
    angle = 2.0 * np.pi * ((b[:, None] * b[None, :]) % LANE) / LANE
    w0 = np.concatenate([np.cos(angle[:, :65]), np.sin(angle[:, 1:64])], axis=1)
    weight = np.full((LANE,), 2.0)
    weight[0] = weight[64] = 1.0
    b0 = (w0 * weight[None, :]).T / LON
    wf = np.stack(fwd).astype(np.float32)
    wb = np.stack(back).astype(np.float32)
    wz = np.stack([w0, b0]).astype(np.float32)
    sines = np.zeros((8, LANE))
    freq0 = np.concatenate([np.arange(65), np.arange(1, 64)]) * 9
    sines[0] = np.sin(np.pi * freq0 / LON) ** 2 * CUT
    for r in range(1, 5):
        sines[r] = np.sin(np.pi * (9 * b + r) / LON) ** 2 * CUT
    lat = (np.arange(NLAT * ROWS, dtype=np.float32) + np.float32(0.5)) * np.float32(
        math.pi / (NLAT * ROWS)
    ) - np.float32(0.5 * math.pi)
    csq = np.cos(lat.astype(np.float64)).astype(np.float32) ** 2
    csq = np.broadcast_to(csq.reshape(NLAT, ROWS, 1), (NLAT, ROWS, LANE)).astype(np.float32)
    return wf, wb, wz, sines.astype(np.float32), np.ascontiguousarray(csq)


def east_west(x):
    return pltpu.roll(x, LON - 1, 1) - pltpu.roll(x, 1, 1)


def first_kernel(
    u_hbm, v_hbm, t_hbm, p_hbm, a_hbm, b_hbm, terr_hbm, csq_hbm, sin_hbm, wf_hbm, wb_hbm, wz_hbm,
    height, east, north, t_out, p_out, a_out, b_out, geo_off,
    fields, terr, csq, sines, wf32, wb32, wz32, wf, wb, wz,
    cum, logmid, halo_t, halo_p, damp,
    s_own, s_pair, s_chip, s_recv, pre, pre_pair,
    d_own, d_pair, d_chip, d_recv, geo_pair,
    y4, y1, z4, z1,
    load_sem, halo_s, halo_r, out_s, out_r,
    bp_s, bp_r, bz_s, bz_r, bq_s, bq_r, be_s, be_r,
    cp_s, cp_r, cz_s, cz_r, cq_s, cq_r, ce_s, ce_r,
):
    la, le = lax.axis_index("lat"), lax.axis_index("lev")
    chip, core = le // 2, le % 2
    other = 1 - core
    up, down = (la + 1) % NLAT, (la + NLAT - 1) % NLAT
    pair_dev = (la, chip * 2 + other)
    side_lat = (la + NLAT - 1 + 2 * core) % NLAT
    cross_dev = (side_lat, chip * 2 + other)
    side_dev = (side_lat, le)
    core_f = core.astype(F32)
    other_f = other.astype(F32)

    def remote(src, dst, send, recv, dev):
        return pltpu.make_async_remote_copy(
            src_ref=src, dst_ref=dst, send_sem=send, recv_sem=recv, device_id=dev, device_id_type=MESH
        )

    ins = (u_hbm, v_hbm, t_hbm, p_hbm, a_hbm, b_hbm)
    load = [
        pltpu.make_async_copy(ins[f], fields.at[f, pl.ds(1, ROWS)], load_sem.at[f]) for f in range(6)
    ]
    load += [
        pltpu.make_async_copy(terr_hbm, terr, load_sem.at[6]),
        pltpu.make_async_copy(csq_hbm.at[la], csq, load_sem.at[7]),
        pltpu.make_async_copy(sin_hbm, sines, load_sem.at[8]),
        pltpu.make_async_copy(wf_hbm, wf32, load_sem.at[9]),
        pltpu.make_async_copy(wb_hbm, wb32, load_sem.at[10]),
        pltpu.make_async_copy(wz_hbm, wz32, load_sem.at[11]),
    ]

    barrier = pltpu.get_barrier_semaphore()
    partners = [(up, le), (down, le), pair_dev, cross_dev]
    partners += [(la, ((chip + d) % CHIPS) * 2 + core) for d in range(1, CHIPS)]
    for dev in partners:
        pl.semaphore_signal(barrier, inc=1, device_id=dev, device_id_type=MESH)
    for f in (2, 3, 0, 1):
        load[f].start()
    pl.semaphore_wait(barrier, len(partners))

    halo = {}
    for f in (2, 3, 0, 1, 4, 5):
        halo[f, 0] = remote(
            ins[f].at[ROWS - 1], fields.at[f, 0], halo_s.at[f, 0], halo_r.at[f, 0], (up, le)
        )
        halo[f, 1] = remote(
            ins[f].at[0], fields.at[f, ROWS + 1], halo_s.at[f, 1], halo_r.at[f, 1], (down, le)
        )
        halo[f, 0].start()
        halo[f, 1].start()
    for f in (4, 5, 6, 7, 8, 9, 10, 11):
        load[f].start()

    row = lax.broadcasted_iota(jnp.int32, (LEVS, LON), 0)

    def halves(x):
        hi = x.astype(BF16)
        return hi, (x - hi.astype(F32)).astype(BF16)

    def run_down(x):
        for s in (1, 2, 4):
            x = x + jnp.where(row >= s, pltpu.roll(x, s, 0), 0.0)
        return x

    def run_up(x):
        for s in (1, 2, 4):
            x = x + jnp.where(row < LEVS - s, pltpu.roll(x, LEVS - s, 0), 0.0)
        return x

    def advected(f, j):
        x = fields[f, j + 1]
        merid = fields[f, j + 2] - fields[f, j]
        return x - COURANT * (fields[0, j + 1] * east_west(x) + fields[1, j + 1] * merid)

    def halo_ready(f):
        halo[f, 0].wait_recv()
        halo[f, 1].wait_recv()

        @pl.when(la == 0)
        def _():
            fields[f, 0] = fields[f, 1]

        @pl.when(la == NLAT - 1)
        def _():
            fields[f, ROWS + 1] = fields[f, ROWS]

    def column_row(j):
        t_out[j] = advected(2, j)
        p = advected(3, j)
        p_out[j] = p
        c = run_down(p)
        cum[j + 1] = c
        s_own[j] = c[LEVS - 1 :, :]

    def span(k):
        if k == EDGE:
            return (ROWS - 1) * core, (ROWS - 1) * other, 1
        start, n = INTERIOR[k]
        return start + n * core, start + n * other, n

    def chunk_rows(k, body):
        if k == EDGE:
            body(0)
            body(ROWS - 1)
        else:
            start, n = INTERIOR[k]

            @pl.loop(start, start + 2 * n)
            def _(j):
                body(j)

    def scan(k, own, pair, total, recv, result, result_pair, sign, base, ps, pr, zs, zr, qs, qr, es, er):
        mine, theirs, n = span(k)
        mine_s, theirs_s = pl.ds(mine, n), pl.ds(theirs, n)
        to_pair = remote(own.at[theirs_s], pair.at[theirs_s], ps.at[k], pr.at[k], pair_dev)
        from_pair = remote(own.at[mine_s], pair.at[mine_s], ps.at[k], pr.at[k], pair_dev)
        share = remote(
            result_pair.at[mine_s], result.at[pl.ds(mine + 1, n)], qs.at[k], qr.at[k], pair_dev
        )
        shared = remote(
            result_pair.at[theirs_s], result.at[pl.ds(theirs + 1, n)], qs.at[k], qr.at[k], pair_dev
        )
        hops = {}
        for d in (2, 1, 3):
            hops[d] = remote(
                total.at[mine_s], recv.at[d - 1, mine_s], zs.at[k, d - 1], zr.at[k, d - 1],
                (la, ((chip + CHIPS + sign * d) % CHIPS) * 2 + core),
            )
        if sign > 0:
            sends = {d: chip + d < CHIPS for d in hops}
            gets = {d: chip >= d for d in hops}
        else:
            sends = {d: chip >= d for d in hops}
            gets = {d: chip + d < CHIPS for d in hops}
        edges = []
        if k == EDGE:
            slot = (ROWS + 1) * other
            edges = [
                remote(result.at[mine + 1], result.at[slot], es.at[0], er.at[other], side_dev),
                remote(result_pair.at[mine], result.at[slot], es.at[1], er.at[other], cross_dev),
            ]

        def begin():
            to_pair.start()

        def middle():
            from_pair.wait_recv()
            total[mine_s] = own[mine_s] + pair[mine_s]
            for d in hops:
                pl.when(sends[d])(hops[d].start)

        def end():
            acc = base(mine, n)
            result[pl.ds(mine + 1, n)] = acc
            for d in hops:

                @pl.when(gets[d])
                def _():
                    hops[d].wait_recv()
                    result[pl.ds(mine + 1, n)] = result[pl.ds(mine + 1, n)] + recv[d - 1, mine_s]

            acc = result[pl.ds(mine + 1, n)]
            mine_f, pair_f = (core_f, other_f) if sign > 0 else (other_f, core_f)
            result_pair[mine_s] = acc + pair_f * own[mine_s]
            share.start()
            result[pl.ds(mine + 1, n)] = acc + mine_f * pair[mine_s]
            for e in edges:
                e.start()

        def finish():
            shared.wait_recv()

        def edge_ready():
            for side in range(2):
                remote(
                    result.at[(ROWS + 1) * side], result.at[(ROWS + 1) * side],
                    es.at[0], er.at[side], side_dev,
                ).wait_recv()

        def drain():
            to_pair.wait_send()
            share.wait_send()
            for d in hops:
                pl.when(sends[d])(hops[d].wait_send)
            for e in edges:
                e.wait_send()

        return begin, middle, end, finish, edge_ready, drain

    def base_top(mine, n):
        return jnp.full((n, 1, LON), TOP, F32)

    def base_terrain(mine, n):
        return jnp.stack([terr[pl.ds(mine + i, 1), :] for i in range(n)], 0)

    top = [
        scan(
            k, s_own, s_pair, s_chip, s_recv, pre, pre_pair, 1, base_top,
            bp_s, bp_r, bz_s, bz_r, bq_s, bq_r, be_s, be_r,
        )
        for k in range(NCHUNK)
    ]
    bottom = [
        scan(
            k, d_own, d_pair, d_chip, d_recv, geo_off, geo_pair, -1, base_terrain,
            cp_s, cp_r, cz_s, cz_r, cq_s, cq_r, ce_s, ce_r,
        )
        for k in range(NCHUNK)
    ]

    def thickness(i, temp):
        base = pre[i]
        lp = jnp.log(base + cum[i])
        above = jnp.where(row == 0, jnp.log(base), pltpu.roll(lp, 1, 0))
        depth = GAS * temp * (lp - above)
        below = run_up(depth)
        height[i] = below - 0.5 * depth
        logmid[i] = 0.5 * (lp + above)
        return below[:1, :]

    def thickness_row(j):
        d_own[j] = thickness(j + 1, t_out[j])

    def gradient_row(j):
        pull = GAS * t_out[j]
        east[j] = east[j] - GRAD * (east_west(height[j + 1]) + pull * east_west(logmid[j + 1]))
        north[j] = north[j] - GRAD * (
            (height[j + 2] - height[j]) + pull * (logmid[j + 2] - logmid[j])
        )

    for f in (2, 3, 0, 1):
        load[f].wait()
    for k in range(EDGE):
        chunk_rows(k, column_row)
        top[k][0]()
    for k in range(EDGE):
        top[k][1]()

    load[4].wait()
    load[5].wait()

    def tracers(j):
        a_out[j] = advected(4, j)
        b_out[j] = advected(5, j)

    @pl.loop(1, ROWS // 2)
    def _(j):
        tracers(j)

    halo_ready(2)
    halo_ready(3)
    column_row(0)
    column_row(ROWS - 1)
    top[EDGE][0]()
    out_copies = []
    for n, (src, dst) in enumerate(((t_out, halo_t), (p_out, halo_p))):
        out_copies.append(
            remote(src.at[ROWS - 1], dst.at[0], out_s.at[n, 0], out_r.at[n, 0], (up, le))
        )
        out_copies.append(remote(src.at[0], dst.at[1], out_s.at[n, 1], out_r.at[n, 1], (down, le)))
    for c in out_copies:
        c.start()

    @pl.loop(ROWS // 2, ROWS - 1)
    def _(j):
        tracers(j)

    top[EDGE][1]()

    load[7].wait()
    load[8].wait()

    @pl.loop(0, ROWS)
    def _(j):
        c = csq[pl.ds(j, 1), :]
        at = pl.ds(pl.multiple_of(j * LEVS, LEVS), LEVS)
        for r in range(5):
            d = c / jnp.maximum(c, sines[r : r + 1, :])
            damp[r, at, :] = jnp.broadcast_to(d, (LEVS, LANE))

    cos9 = [math.cos(2.0 * math.pi * i / 9) for i in range(9)]
    sin9 = [math.sin(2.0 * math.pi * i / 9) for i in range(9)]

    def forward_nine(i):
        at = pl.ds(pl.multiple_of(i * 16, 16), 16)
        for f in range(2):
            x = jnp.concatenate([advected(f, 2 * i), advected(f, 2 * i + 1)], axis=0)
            xs = [x[:, LANE * a : LANE * (a + 1)] for a in range(9)]
            even = [xs[a] + xs[9 - a] for a in range(1, 5)]
            odd = [xs[a] - xs[9 - a] for a in range(1, 5)]
            y1[f, 0, at, :], y1[f, 1, at, :] = halves(xs[0] + ((even[0] + even[1]) + (even[2] + even[3])))
            for r in range(1, 5):
                re, im = xs[0], None
                for a in range(1, 5):
                    re = re + cos9[(a * r) % 9] * even[a - 1]
                    term = -sin9[(a * r) % 9] * odd[a - 1]
                    im = term if im is None else im + term
                hi, lo = halves(re)
                y4[f, r - 1, 0, at, :LANE], y4[f, r - 1, 1, at, :LANE] = hi, lo
                hi, lo = halves(im)
                y4[f, r - 1, 0, at, LANE:], y4[f, r - 1, 1, at, LANE:] = hi, lo

    def dot3(xh, xl, wh, wl):
        def mm(x, w):
            return jnp.dot(x, w, preferred_element_type=F32)

        return mm(xh, wh) + (mm(xl, wh) + mm(xh, wl))

    def spectrum(n):
        f, r = n // 4, n % 4
        x = dot3(y4[f, r, 0], y4[f, r, 1], wf[r, 0], wf[r, 1])
        d = damp[r + 1]
        xh, xl = halves(x * jnp.concatenate([d, d], axis=1))
        z4[f, r] = dot3(xh, xl, wb[r, 0], wb[r, 1])

    def spectrum_zero(f):
        x = dot3(y1[f, 0], y1[f, 1], wz[0], wz[1])
        xh, xl = halves(x * damp[0])
        z1[f] = dot3(xh, xl, wz[2], wz[3])

    def backward_nine(i):
        at = pl.ds(pl.multiple_of(i * 16, 16), 16)
        for f, dst in ((0, east), (1, north)):
            z0 = z1[f, at, :]
            re = [z4[f, r, at, :LANE] for r in range(4)]
            im = [z4[f, r, at, LANE:] for r in range(4)]
            outs = [None] * 9
            outs[0] = z0 + ((re[0] + re[1]) + (re[2] + re[3]))
            for a in range(1, 5):
                even, odd = z0, None
                for r in range(1, 5):
                    even = even + cos9[(a * r) % 9] * re[r - 1]
                    term = sin9[(a * r) % 9] * im[r - 1]
                    odd = term if odd is None else odd + term
                outs[a], outs[9 - a] = even - odd, even + odd
            for a in range(9):
                dst[2 * i, :, LANE * a : LANE * (a + 1)] = outs[a][:LEVS]
                dst[2 * i + 1, :, LANE * a : LANE * (a + 1)] = outs[a][LEVS:]

    for n in (9, 10, 11):
        load[n].wait()

    @pl.loop(0, 4)
    def _(r):
        @pl.loop(0, 4)
        def _(i):
            at = pl.ds(pl.multiple_of(i * 64, 64), 64)
            wf[r, 0, at, :], wf[r, 1, at, :] = halves(wf32[r, at, :])
            wb[r, 0, at, :], wb[r, 1, at, :] = halves(wb32[r, at, :])

    wz[0], wz[1] = halves(wz32[0])
    wz[2], wz[3] = halves(wz32[1])

    halo_ready(0)
    halo_ready(1)

    @pl.loop(0, ROWS // 2)
    def _(i):
        forward_nine(i)

    load[6].wait()

    for k in range(EDGE):
        top[k][2]()
        top[k][3]()
        chunk_rows(k, thickness_row)
        bottom[k][0]()
        if k == 0:
            spectrum_zero(0)
            spectrum_zero(1)
        else:
            pl.loop(0, 1)(spectrum)
        bottom[k][1]()
    top[EDGE][2]()
    top[EDGE][3]()
    chunk_rows(EDGE, thickness_row)
    bottom[EDGE][0]()
    halo_ready(4)
    halo_ready(5)
    tracers(0)
    tracers(ROWS - 1)
    bottom[EDGE][1]()

    pl.loop(1, 8)(spectrum)

    @pl.loop(0, ROWS // 2)
    def _(i):
        backward_nine(i)

    for c in out_copies:
        c.wait_recv()
    top[EDGE][4]()
    for side in range(2):
        i = (ROWS + 1) * side
        cum[i] = run_down(halo_p[side])
        thickness(i, halo_t[side])

    @pl.when(la == 0)
    def _():
        height[0] = height[1]
        logmid[0] = logmid[1]

    @pl.when(la == NLAT - 1)
    def _():
        height[ROWS + 1] = height[ROWS]
        logmid[ROWS + 1] = logmid[ROWS]

    @pl.loop(0, ROWS)
    def _(j):
        gradient_row(j)

    for k in range(NCHUNK):
        bottom[k][2]()
    for k in range(NCHUNK):
        bottom[k][3]()
    bottom[EDGE][4]()

    @pl.when(la == 0)
    def _():
        geo_off[0] = geo_off[1]

    @pl.when(la == NLAT - 1)
    def _():
        geo_off[ROWS + 1] = geo_off[ROWS]

    for k in range(NCHUNK):
        top[k][5]()
        bottom[k][5]()
    for key in halo:
        halo[key].wait_send()
    for c in out_copies:
        c.wait_send()


def second_kernel(
    height, east, north, t_out, p_out, a_out, b_out, geo_off,
    east_hbm, north_hbm, t_hbm, p_hbm, a_hbm, b_hbm, geo_hbm,
    east_buf, north_buf, geo_buf, sem,
):
    copies = [
        pltpu.make_async_copy(src, dst, sem.at[n])
        for n, (src, dst) in enumerate(((t_out, t_hbm), (p_out, p_hbm), (a_out, a_hbm), (b_out, b_hbm)))
    ]
    for c in copies:
        c.start()
    part = 8
    for q in range(ROWS // part):

        @pl.loop(part * q, part * (q + 1))
        def _(j):
            off = geo_off[j + 1]
            geo_buf[j] = height[j + 1] + off
            east_buf[j] = east[j] - GRAD * east_west(off)
            north_buf[j] = north[j] - GRAD * (geo_off[j + 2] - geo_off[j])

        for m, (src, dst) in enumerate(((east_buf, east_hbm), (north_buf, north_hbm), (geo_buf, geo_hbm))):
            rows = pl.ds(part * q, part)
            c = pltpu.make_async_copy(src.at[rows], dst.at[rows], sem.at[4 + 3 * q + m])
            c.start()
            copies.append(c)
    for c in copies:
        c.wait()


def shards(u, v, t, p, a, b, terrain):
    wf, wb, wz, sines, csq = (jnp.asarray(x) for x in tables())
    ins = [u, v, t, p, a, b, terrain, csq, sines, wf, wb, wz]
    ins = [pltpu.with_memory_space_constraint(x, pltpu.HBM) for x in ins]
    full = (ROWS, LEVS, LON)
    wide = (ROWS + 2, LEVS, LON)
    line = (ROWS, 1, LON)
    line_wide = (ROWS + 2, 1, LON)
    dma = pltpu.SemaphoreType.DMA
    scan_sems = [
        dma((NCHUNK,)), dma((NCHUNK,)), dma((NCHUNK, 3)), dma((NCHUNK, 3)),
        dma((NCHUNK,)), dma((NCHUNK,)), dma((2,)), dma((2,)),
    ]
    mids = pl.pallas_call(
        first_kernel,
        out_shape=[pltpu.VMEM(wide, F32)] + [pltpu.VMEM(full, F32)] * 6 + [pltpu.VMEM(line_wide, F32)],
        in_specs=[pl.BlockSpec(memory_space=pltpu.HBM)] * len(ins),
        out_specs=[pl.BlockSpec(memory_space=pltpu.VMEM)] * 8,
        scratch_shapes=[
            pltpu.VMEM((6,) + wide, F32),
            pltpu.VMEM((ROWS, LON), F32),
            pltpu.VMEM((ROWS, LANE), F32),
            pltpu.VMEM((8, LANE), F32),
            pltpu.VMEM((4, 256, 256), F32),
            pltpu.VMEM((4, 256, 256), F32),
            pltpu.VMEM((2, LANE, LANE), F32),
            pltpu.VMEM((4, 2, 256, 256), BF16),
            pltpu.VMEM((4, 2, 256, 256), BF16),
            pltpu.VMEM((4, LANE, LANE), BF16),
            pltpu.VMEM(wide, F32),
            pltpu.VMEM(wide, F32),
            pltpu.VMEM((2, LEVS, LON), F32),
            pltpu.VMEM((2, LEVS, LON), F32),
            pltpu.VMEM((5, ROWS * LEVS, LANE), F32),
            pltpu.VMEM(line, F32),
            pltpu.VMEM(line, F32),
            pltpu.VMEM(line, F32),
            pltpu.VMEM((3,) + line, F32),
            pltpu.VMEM(line_wide, F32),
            pltpu.VMEM(line, F32),
            pltpu.VMEM(line, F32),
            pltpu.VMEM(line, F32),
            pltpu.VMEM(line, F32),
            pltpu.VMEM((3,) + line, F32),
            pltpu.VMEM(line, F32),
            pltpu.VMEM((2, 4, 2, ROWS * LEVS, 2 * LANE), BF16),
            pltpu.VMEM((2, 2, ROWS * LEVS, LANE), BF16),
            pltpu.VMEM((2, 4, ROWS * LEVS, 2 * LANE), F32),
            pltpu.VMEM((2, ROWS * LEVS, LANE), F32),
            dma((12,)), dma((6, 2)), dma((6, 2)), dma((2, 2)), dma((2, 2)),
        ]
        + scan_sems
        + scan_sems,
        compiler_params=pltpu.CompilerParams(
            collective_id=0, has_side_effects=True, vmem_limit_bytes=40 << 20
        ),
    )(*ins)
    outs = pl.pallas_call(
        second_kernel,
        out_shape=[jax.ShapeDtypeStruct(full, F32)] * 7,
        in_specs=[pl.BlockSpec(memory_space=pltpu.VMEM)] * 8,
        out_specs=[pl.BlockSpec(memory_space=pltpu.HBM)] * 7,
        scratch_shapes=[pltpu.VMEM(full, F32)] * 3 + [dma((13,))],
        compiler_params=pltpu.CompilerParams(vmem_limit_bytes=20 << 20),
    )(*mids)
    return tuple(outs)


def solution(mesh):
    field = P("lat", "lev", None)
    return jax.shard_map(
        shards,
        mesh=mesh,
        in_specs=(field,) * 6 + (P("lat", None),),
        out_specs=(field,) * 7,
        check_vma=False,
    )
```

profile of v0, /device:TPU:1, one launch (start us, length us, event | category | flops | bytes accessed | tf_op | source)
XLA Modules:
  0.0 43.2 jit_solution(79138914570026953)
XLA Ops:
  0.6 39.2 %shard_map.171 = (f32[26,8,1152]{2,1,0:T(8,128)S(1)}, f32[24,8,1152]{2,1,0:T(8,128)S(1)}, f32[24,8,1152]{2,1,0:T(8,128)S(1)}, f32[24,8,1152]{2,1,0:T(8,128)S(1)}...) custom-call(f32[24,8,1152]{2,1,0:T(8,128)} %u_hbm.1, ...), custom_call_target="tpu_custom_call" | custom-call | tf_op jit(solution)/shard_map/pallas_call | solution.py:553
  39.9 3.3 %shard_map.172 = (f32[24,8,1152]{2,1,0:T(8,128)}, f32[24,8,1152]{2,1,0:T(8,128)}, f32[24,8,1152]{2,1,0:T(8,128)}, f32[24,8,1152]{2,1,0:T(8,128)}, f32[24,8,1152]...) custom-call(f32[26,8,1152]{2,1,0:T(8,128)S(1)} %get-tuple-element.15.height, ...), custom_call_target="tpu_custom_call" | custom-call | tf_op jit(solution)/shard_map/pallas_call | solution.py:597
where the time goes:
time: 43.3 us; the launch traced here: 43.2 us
  Pallas kernels  42.6 us (98%)
  between operations  0.64 us (1%)
    pallas_call x1, Pallas kernels, shards(): pl.pallas_call(first_kernel, out_shape=[pltpu.VMEM(wide, F32)] + [pltpu.V...  39.2 us
    pallas_call x1, Pallas kernels, shards(): pl.pallas_call(second_kernel, out_shape=[jax.ShapeDtypeStruct(full, F32)]...  3.32 us

commit v1 on v0

--- a/solution.py
+++ b/solution.py
@@ -23,6 +23,11 @@
 TOP = 1.0
 CUT = 0.5
 
+POLAR = sum(
+    math.cos(((ROWS * band + ROWS - 0.5) / (NLAT * ROWS) - 0.5) * math.pi) ** 2 < CUT
+    or math.cos(((ROWS * band + 0.5) / (NLAT * ROWS) - 0.5) * math.pi) ** 2 < CUT
+    for band in range(NLAT // 2)
+)
 INTERIOR = ((1, 6), (13, 5))
 EDGE = len(INTERIOR)
 NCHUNK = EDGE + 1
@@ -67,13 +72,13 @@
     u_hbm, v_hbm, t_hbm, p_hbm, a_hbm, b_hbm, terr_hbm, csq_hbm, sin_hbm, wf_hbm, wb_hbm, wz_hbm,
     height, east, north, t_out, p_out, a_out, b_out, geo_off,
     fields, terr, csq, sines, wf32, wb32, wz32, wf, wb, wz,
-    cum, logmid, halo_t, halo_p, damp,
+    cum, logmid, halo_t, halo_p, damp, pair_t, pair_c,
     s_own, s_pair, s_chip, s_recv, pre, pre_pair,
     d_own, d_pair, d_chip, d_recv, geo_pair,
     y4, y1, z4, z1,
-    load_sem, halo_s, halo_r, out_s, out_r,
+    ready, load_sem, halo_s, halo_r, out_s, out_r, both_s, both_r,
     bp_s, bp_r, bz_s, bz_r, bq_s, bq_r, be_s, be_r,
-    cp_s, cp_r, cz_s, cz_r, cq_s, cq_r, ce_s, ce_r,
+    cz_s, cz_r, cq_s, cq_r, ce_s, ce_r,
 ):
     la, le = lax.axis_index("lat"), lax.axis_index("lev")
     chip, core = le // 2, le % 2
@@ -83,6 +88,8 @@
     side_lat = (la + NLAT - 1 + 2 * core) % NLAT
     cross_dev = (side_lat, chip * 2 + other)
     side_dev = (side_lat, le)
+    has_up, has_down = la < NLAT - 1, la > 0
+    has_side = jnp.where(core == 0, la, NLAT - 1 - la) > 0
     core_f = core.astype(F32)
     other_f = other.astype(F32)
 
@@ -105,13 +112,18 @@
     ]
 
     barrier = pltpu.get_barrier_semaphore()
-    partners = [(up, le), (down, le), pair_dev, cross_dev]
-    partners += [(la, ((chip + d) % CHIPS) * 2 + core) for d in range(1, CHIPS)]
-    for dev in partners:
-        pl.semaphore_signal(barrier, inc=1, device_id=dev, device_id_type=MESH)
-    for f in (2, 3, 0, 1):
+    upper = chip < CHIPS // 2
+    others = [(chip + d) % CHIPS for d in range(1, CHIPS)]
+    greet = [(la >= 0, pair_dev), (has_up, (up, le)), (has_down, (down, le)), (has_side, cross_dev)]
+    greet += [(upper | (c >= CHIPS // 2), (la, c * 2 + core)) for c in others]
+    for there, dev in greet:
+
+        @pl.when(there)
+        def _():
+            pl.semaphore_signal(barrier, inc=1, device_id=dev, device_id_type=MESH)
+
+    for f in (3, 0, 1, 2):
         load[f].start()
-    pl.semaphore_wait(barrier, len(partners))
 
     halo = {}
     for f in (2, 3, 0, 1, 4, 5):
@@ -121,10 +133,27 @@
         halo[f, 1] = remote(
             ins[f].at[0], fields.at[f, ROWS + 1], halo_s.at[f, 1], halo_r.at[f, 1], (down, le)
         )
-        halo[f, 0].start()
-        halo[f, 1].start()
-    for f in (4, 5, 6, 7, 8, 9, 10, 11):
-        load[f].start()
+
+    seam = la == NLAT // 2 - 1
+
+    def halo_start(f):
+        pl.when(has_up & ~seam)(halo[f, 0].start)
+        pl.when(has_down)(halo[f, 1].start)
+
+    def enter():
+        near = has_up.astype(jnp.int32) + has_down.astype(jnp.int32) + has_side.astype(jnp.int32)
+        pl.semaphore_wait(barrier, near + jnp.where(upper, 2, 4))
+
+        @pl.when(~upper)
+        def _():
+            for c in range(CHIPS // 2):
+                pl.semaphore_signal(ready, inc=1, device_id=(la, c * 2 + core), device_id_type=MESH)
+
+        for f in (3, 2):
+            pl.when(has_up)(halo[f, 0].start)
+            pl.when(has_down)(halo[f, 1].start)
+
+    enter()
 
     row = lax.broadcasted_iota(jnp.int32, (LEVS, LON), 0)
 
@@ -148,8 +177,13 @@
         return x - COURANT * (fields[0, j + 1] * east_west(x) + fields[1, j + 1] * merid)
 
     def halo_ready(f):
-        halo[f, 0].wait_recv()
-        halo[f, 1].wait_recv()
+        @pl.when(has_down)
+        def _():
+            halo[f, 0].wait_recv()
+
+        @pl.when(has_up)
+        def _():
+            halo[f, 1].wait_recv()
 
         @pl.when(la == 0)
         def _():
@@ -159,8 +193,10 @@
         def _():
             fields[f, ROWS + 1] = fields[f, ROWS]
 
-    def column_row(j):
+    def column_t(j):
         t_out[j] = advected(2, j)
+
+    def column_p(j):
         p = advected(3, j)
         p_out[j] = p
         c = run_down(p)
@@ -180,15 +216,16 @@
         else:
             start, n = INTERIOR[k]
 
-            @pl.loop(start, start + 2 * n)
+            @pl.loop(start, start + 2 * n, unroll=2)
             def _(j):
                 body(j)
 
-    def scan(k, own, pair, total, recv, result, result_pair, sign, base, ps, pr, zs, zr, qs, qr, es, er):
+    def scan(k, own, pair, total, recv, result, result_pair, sign, base, zs, zr, qs, qr, es, er, ps=None, pr=None):
         mine, theirs, n = span(k)
         mine_s, theirs_s = pl.ds(mine, n), pl.ds(theirs, n)
-        to_pair = remote(own.at[theirs_s], pair.at[theirs_s], ps.at[k], pr.at[k], pair_dev)
-        from_pair = remote(own.at[mine_s], pair.at[mine_s], ps.at[k], pr.at[k], pair_dev)
+        if ps is not None:
+            to_pair = remote(own.at[theirs_s], pair.at[theirs_s], ps.at[k], pr.at[k], pair_dev)
+            from_pair = remote(own.at[mine_s], pair.at[mine_s], ps.at[k], pr.at[k], pair_dev)
         share = remote(
             result_pair.at[mine_s], result.at[pl.ds(mine + 1, n)], qs.at[k], qr.at[k], pair_dev
         )
@@ -219,10 +256,18 @@
             to_pair.start()
 
         def middle():
-            from_pair.wait_recv()
+            if ps is not None:
+                from_pair.wait_recv()
             total[mine_s] = own[mine_s] + pair[mine_s]
+            if sign > 0:
+                pl.when(chip % 2 == 0)(hops[1].start)
+            else:
+                for d in hops:
+                    pl.when(sends[d])(hops[d].start)
+
+        def across():
             for d in hops:
-                pl.when(sends[d])(hops[d].start)
+                pl.when(upper & sends[d] & ((chip + d) >= CHIPS // 2))(hops[d].start)
 
         def end():
             acc = base(mine, n)
@@ -240,27 +285,27 @@
             share.start()
             result[pl.ds(mine + 1, n)] = acc + mine_f * pair[mine_s]
             for e in edges:
-                e.start()
+                pl.when(has_side)(e.start)
 
         def finish():
             shared.wait_recv()
 
         def edge_ready():
-            for side in range(2):
-                remote(
-                    result.at[(ROWS + 1) * side], result.at[(ROWS + 1) * side],
-                    es.at[0], er.at[side], side_dev,
-                ).wait_recv()
+            for side, there in ((0, has_down), (1, has_up)):
+                slot = (ROWS + 1) * side
+                c = remote(result.at[slot], result.at[slot], es.at[0], er.at[side], side_dev)
+                pl.when(there)(c.wait_recv)
 
         def drain():
-            to_pair.wait_send()
+            if ps is not None:
+                to_pair.wait_send()
             share.wait_send()
             for d in hops:
                 pl.when(sends[d])(hops[d].wait_send)
             for e in edges:
-                e.wait_send()
-
-        return begin, middle, end, finish, edge_ready, drain
+                pl.when(has_side)(e.wait_send)
+
+        return begin, middle, end, finish, edge_ready, drain, across
 
     def base_top(mine, n):
         return jnp.full((n, 1, LON), TOP, F32)
@@ -271,14 +316,14 @@
     top = [
         scan(
             k, s_own, s_pair, s_chip, s_recv, pre, pre_pair, 1, base_top,
-            bp_s, bp_r, bz_s, bz_r, bq_s, bq_r, be_s, be_r,
+            bz_s, bz_r, bq_s, bq_r, be_s, be_r, bp_s, bp_r,
         )
         for k in range(NCHUNK)
     ]
     bottom = [
         scan(
             k, d_own, d_pair, d_chip, d_recv, geo_off, geo_pair, -1, base_terrain,
-            cp_s, cp_r, cz_s, cz_r, cq_s, cq_r, ce_s, ce_r,
+            cz_s, cz_r, cq_s, cq_r, ce_s, ce_r,
         )
         for k in range(NCHUNK)
     ]
@@ -303,102 +348,173 @@
             (height[j + 2] - height[j]) + pull * (logmid[j + 2] - logmid[j])
         )
 
-    for f in (2, 3, 0, 1):
-        load[f].wait()
-    for k in range(EDGE):
-        chunk_rows(k, column_row)
-        top[k][0]()
-    for k in range(EDGE):
-        top[k][1]()
-
-    load[4].wait()
-    load[5].wait()
+    def both(k):
+        _, theirs, n = span(k)
+        at = pl.ds(theirs, n)
+        return (
+            remote(cum.at[pl.ds(theirs + 1, n)], pair_c.at[at], both_s.at[k, 0], both_r.at[k, 0], pair_dev),
+            remote(t_out.at[at], pair_t.at[at], both_s.at[k, 1], both_r.at[k, 1], pair_dev),
+        )
+
+    def pair_row(j):
+        base = pre_pair[j]
+        lp = jnp.log(base + pair_c[j])
+        above = jnp.where(row == 0, jnp.log(base), pltpu.roll(lp, 1, 0))
+        depth = GAS * pair_t[j] * (lp - above)
+        d_pair[j] = jnp.sum(depth, axis=0, keepdims=True)
+
+    def mine_rows(k):
+        mine, _, n = span(k)
+
+        @pl.loop(0, n, unroll=n)
+        def _(i):
+            thickness_row(mine + i)
+            pair_row(mine + i)
+
+    def their_rows(k):
+        _, theirs, n = span(k)
+
+        @pl.loop(0, n, unroll=n)
+        def _(i):
+            thickness_row(theirs + i)
 
     def tracers(j):
         a_out[j] = advected(4, j)
         b_out[j] = advected(5, j)
 
-    @pl.loop(1, ROWS // 2)
-    def _(j):
-        tracers(j)
-
+    def inner_tracers():
+        @pl.loop(1, ROWS - 1, unroll=2)
+        def _(j):
+            tracers(j)
+
+    for f in (3, 0, 1):
+        load[f].wait()
+    for f in (4, 5, 6, 7, 8, 9, 10, 11):
+        load[f].start()
+    for k in range(EDGE):
+        chunk_rows(k, column_p)
+        top[k][0]()
+    load[2].wait()
+    pairs = [both(k) for k in range(NCHUNK)]
+    for k in range(EDGE):
+        chunk_rows(k, column_t)
+        for c in pairs[k]:
+            c.start()
+    for k in range(EDGE):
+        top[k][1]()
+    halo_start(0)
+    halo_start(1)
+
+    @pl.when(upper)
+    def _():
+        pl.semaphore_wait(ready, CHIPS // 2)
+
+    for k in range(EDGE):
+        top[k][6]()
+
+    halo_ready(3)
+    column_p(0)
+    column_p(ROWS - 1)
+    top[EDGE][0]()
     halo_ready(2)
-    halo_ready(3)
-    column_row(0)
-    column_row(ROWS - 1)
-    top[EDGE][0]()
+    column_t(0)
+    column_t(ROWS - 1)
+    for c in pairs[EDGE]:
+        c.start()
     out_copies = []
     for n, (src, dst) in enumerate(((t_out, halo_t), (p_out, halo_p))):
         out_copies.append(
             remote(src.at[ROWS - 1], dst.at[0], out_s.at[n, 0], out_r.at[n, 0], (up, le))
         )
         out_copies.append(remote(src.at[0], dst.at[1], out_s.at[n, 1], out_r.at[n, 1], (down, le)))
-    for c in out_copies:
-        c.start()
-
-    @pl.loop(ROWS // 2, ROWS - 1)
-    def _(j):
-        tracers(j)
-
+    ways = (has_up, has_down)
     top[EDGE][1]()
-
-    load[7].wait()
-    load[8].wait()
-
-    @pl.loop(0, ROWS)
-    def _(j):
-        c = csq[pl.ds(j, 1), :]
-        at = pl.ds(pl.multiple_of(j * LEVS, LEVS), LEVS)
-        for r in range(5):
-            d = c / jnp.maximum(c, sines[r : r + 1, :])
-            damp[r, at, :] = jnp.broadcast_to(d, (LEVS, LANE))
+    top[EDGE][6]()
+    for n, c in enumerate(out_copies):
+        pl.when(ways[n % 2])(c.start)
+
+    @pl.when(seam)
+    def _():
+        halo[0, 0].start()
+        halo[1, 0].start()
+
+    for f in (4, 5):
+        pl.when(has_up)(halo[f, 0].start)
+        pl.when(has_down)(halo[f, 1].start)
+
+    for n in (4, 5, 6, 7, 8, 9, 10, 11):
+        load[n].wait()
+
+    def prepare():
+        @pl.loop(0, ROWS, unroll=4)
+        def _(j):
+            c = csq[pl.ds(j, 1), :]
+            at = pl.ds(pl.multiple_of(j * LEVS, LEVS), LEVS)
+            for r in range(5):
+                d = c / jnp.maximum(c, sines[r : r + 1, :])
+                damp[r, at, :] = jnp.broadcast_to(d, (LEVS, LANE))
+
+        for full, parts in ((wf32, wf), (wb32, wb)):
+
+            @pl.loop(0, 4)
+            def _(r):
+                for i in range(0, 256, 64):
+                    hi, lo = halves(full[r, i : i + 64, :])
+                    parts[r, i : i + 64, :] = hi
+                    parts[r, 256 + i : 320 + i, :] = hi
+                    parts[r, 512 + i : 576 + i, :] = lo
+
+        for n in range(2):
+            hi, lo = halves(wz32[n])
+            wz[n, :LANE, :], wz[n, LANE : 2 * LANE, :], wz[n, 2 * LANE :, :] = hi, hi, lo
 
     cos9 = [math.cos(2.0 * math.pi * i / 9) for i in range(9)]
     sin9 = [math.sin(2.0 * math.pi * i / 9) for i in range(9)]
 
     def forward_nine(i):
-        at = pl.ds(pl.multiple_of(i * 16, 16), 16)
         for f in range(2):
+            at = pl.ds(pl.multiple_of(f * ROWS * LEVS + i * 16, 16), 16)
             x = jnp.concatenate([advected(f, 2 * i), advected(f, 2 * i + 1)], axis=0)
             xs = [x[:, LANE * a : LANE * (a + 1)] for a in range(9)]
             even = [xs[a] + xs[9 - a] for a in range(1, 5)]
             odd = [xs[a] - xs[9 - a] for a in range(1, 5)]
-            y1[f, 0, at, :], y1[f, 1, at, :] = halves(xs[0] + ((even[0] + even[1]) + (even[2] + even[3])))
+            hi, lo = halves(xs[0] + ((even[0] + even[1]) + (even[2] + even[3])))
+            y1[at, :LANE], y1[at, LANE : 2 * LANE], y1[at, 2 * LANE :] = hi, lo, hi
             for r in range(1, 5):
                 re, im = xs[0], None
                 for a in range(1, 5):
                     re = re + cos9[(a * r) % 9] * even[a - 1]
                     term = -sin9[(a * r) % 9] * odd[a - 1]
                     im = term if im is None else im + term
-                hi, lo = halves(re)
-                y4[f, r - 1, 0, at, :LANE], y4[f, r - 1, 1, at, :LANE] = hi, lo
-                hi, lo = halves(im)
-                y4[f, r - 1, 0, at, LANE:], y4[f, r - 1, 1, at, LANE:] = hi, lo
-
-    def dot3(xh, xl, wh, wl):
-        def mm(x, w):
-            return jnp.dot(x, w, preferred_element_type=F32)
-
-        return mm(xh, wh) + (mm(xl, wh) + mm(xh, wl))
-
-    def spectrum(n):
-        f, r = n // 4, n % 4
-        x = dot3(y4[f, r, 0], y4[f, r, 1], wf[r, 0], wf[r, 1])
+                for part, y in ((0, re), (1, im)):
+                    hi, lo = halves(y)
+                    for place, value in ((0, hi), (2, lo), (4, hi)):
+                        place = (place + part) * LANE
+                        y4[r - 1, at, place : place + LANE] = value
+
+    def triple(x):
+        hi, lo = halves(x)
+        return jnp.concatenate([hi, lo, hi], axis=1)
+
+    def mm(x, w):
+        return jnp.dot(x, w, preferred_element_type=F32)
+
+    def spectrum(r):
         d = damp[r + 1]
-        xh, xl = halves(x * jnp.concatenate([d, d], axis=1))
-        z4[f, r] = dot3(xh, xl, wb[r, 0], wb[r, 1])
-
-    def spectrum_zero(f):
-        x = dot3(y1[f, 0], y1[f, 1], wz[0], wz[1])
-        xh, xl = halves(x * damp[0])
-        z1[f] = dot3(xh, xl, wz[2], wz[3])
+        d = jnp.concatenate([d, d], axis=1)
+        d = jnp.concatenate([d, d], axis=0)
+        z4[r] = mm(triple(mm(y4[r], wf[r]) * d), wb[r])
+
+    def spectrum_zero():
+        d = jnp.concatenate([damp[0], damp[0]], axis=0)
+        z1[...] = mm(triple(mm(y1[...], wz[0]) * d), wz[1])
 
     def backward_nine(i):
-        at = pl.ds(pl.multiple_of(i * 16, 16), 16)
         for f, dst in ((0, east), (1, north)):
-            z0 = z1[f, at, :]
-            re = [z4[f, r, at, :LANE] for r in range(4)]
-            im = [z4[f, r, at, LANE:] for r in range(4)]
+            at = pl.ds(pl.multiple_of(f * ROWS * LEVS + i * 16, 16), 16)
+            z0 = z1[at, :]
+            re = [z4[r, at, :LANE] for r in range(4)]
+            im = [z4[r, at, LANE:] for r in range(4)]
             outs = [None] * 9
             outs[0] = z0 + ((re[0] + re[1]) + (re[2] + re[3]))
             for a in range(1, 5):
@@ -412,63 +528,78 @@
                 dst[2 * i, :, LANE * a : LANE * (a + 1)] = outs[a][:LEVS]
                 dst[2 * i + 1, :, LANE * a : LANE * (a + 1)] = outs[a][LEVS:]
 
-    for n in (9, 10, 11):
-        load[n].wait()
-
-    @pl.loop(0, 4)
-    def _(r):
-        @pl.loop(0, 4)
+    polar = (la < POLAR) | (la >= NLAT - POLAR)
+
+    def forward():
+        prepare()
+        halo_ready(0)
+        halo_ready(1)
+
+        @pl.loop(0, ROWS // 2, unroll=2)
         def _(i):
-            at = pl.ds(pl.multiple_of(i * 64, 64), 64)
-            wf[r, 0, at, :], wf[r, 1, at, :] = halves(wf32[r, at, :])
-            wb[r, 0, at, :], wb[r, 1, at, :] = halves(wb32[r, at, :])
-
-    wz[0], wz[1] = halves(wz32[0])
-    wz[2], wz[3] = halves(wz32[1])
-
-    halo_ready(0)
-    halo_ready(1)
-
-    @pl.loop(0, ROWS // 2)
-    def _(i):
-        forward_nine(i)
-
-    load[6].wait()
+            forward_nine(i)
+
+    pl.when(upper)(inner_tracers)
+    pl.when(polar & upper)(forward)
 
     for k in range(EDGE):
         top[k][2]()
-        top[k][3]()
-        chunk_rows(k, thickness_row)
-        bottom[k][0]()
-        if k == 0:
-            spectrum_zero(0)
-            spectrum_zero(1)
-        else:
-            pl.loop(0, 1)(spectrum)
+        for c in pairs[k]:
+            c.wait_recv()
+        mine_rows(k)
         bottom[k][1]()
     top[EDGE][2]()
-    top[EDGE][3]()
-    chunk_rows(EDGE, thickness_row)
-    bottom[EDGE][0]()
+    for c in pairs[EDGE]:
+        c.wait_recv()
+    mine_rows(EDGE)
+    bottom[EDGE][1]()
+    for k in range(NCHUNK):
+        top[k][3]()
+        their_rows(k)
+    pl.when(~upper)(inner_tracers)
+    pl.when(polar & ~upper)(forward)
+
+    @pl.when(polar)
+    def _():
+        spectrum_zero()
+        pl.loop(0, 4)(spectrum)
+
+        @pl.loop(0, ROWS // 2, unroll=2)
+        def _(i):
+            backward_nine(i)
+
+    @pl.when(~polar)
+    def _():
+        @pl.loop(1, ROWS - 1, unroll=2)
+        def _(j):
+            east[j] = advected(0, j)
+            north[j] = advected(1, j)
+
+        halo_ready(0)
+        halo_ready(1)
+        for j in (0, ROWS - 1):
+            east[j] = advected(0, j)
+            north[j] = advected(1, j)
+
+    @pl.loop(1, ROWS - 1, unroll=2)
+    def _(j):
+        gradient_row(j)
+
     halo_ready(4)
     halo_ready(5)
     tracers(0)
     tracers(ROWS - 1)
-    bottom[EDGE][1]()
-
-    pl.loop(1, 8)(spectrum)
-
-    @pl.loop(0, ROWS // 2)
-    def _(i):
-        backward_nine(i)
-
-    for c in out_copies:
-        c.wait_recv()
+
+    for n, c in enumerate(out_copies):
+        pl.when(ways[1 - n % 2])(c.wait_recv)
     top[EDGE][4]()
-    for side in range(2):
-        i = (ROWS + 1) * side
-        cum[i] = run_down(halo_p[side])
-        thickness(i, halo_t[side])
+    for side, there in ((0, has_down), (1, has_up)):
+
+        @pl.when(there)
+        def _():
+            i = (ROWS + 1) * side
+            cum[i] = run_down(halo_p[side])
+            thickness(i, halo_t[side])
 
     @pl.when(la == 0)
     def _():
@@ -480,9 +611,8 @@
         height[ROWS + 1] = height[ROWS]
         logmid[ROWS + 1] = logmid[ROWS]
 
-    @pl.loop(0, ROWS)
-    def _(j):
-        gradient_row(j)
+    gradient_row(0)
+    gradient_row(ROWS - 1)
 
     for k in range(NCHUNK):
         bottom[k][2]()
@@ -501,10 +631,13 @@
     for k in range(NCHUNK):
         top[k][5]()
         bottom[k][5]()
-    for key in halo:
-        halo[key].wait_send()
-    for c in out_copies:
-        c.wait_send()
+    for pair in pairs:
+        for c in pair:
+            c.wait_send()
+    for (f, side), c in halo.items():
+        pl.when(ways[side])(c.wait_send)
+    for n, c in enumerate(out_copies):
+        pl.when(ways[n % 2])(c.wait_send)
 
 
 def second_kernel(
@@ -521,7 +654,7 @@
     part = 8
     for q in range(ROWS // part):
 
-        @pl.loop(part * q, part * (q + 1))
+        @pl.loop(part * q, part * (q + 1), unroll=4)
         def _(j):
             off = geo_off[j + 1]
             geo_buf[j] = height[j + 1] + off
@@ -563,14 +696,16 @@
             pltpu.VMEM((4, 256, 256), F32),
             pltpu.VMEM((4, 256, 256), F32),
             pltpu.VMEM((2, LANE, LANE), F32),
-            pltpu.VMEM((4, 2, 256, 256), BF16),
-            pltpu.VMEM((4, 2, 256, 256), BF16),
-            pltpu.VMEM((4, LANE, LANE), BF16),
+            pltpu.VMEM((4, 3 * 256, 256), BF16),
+            pltpu.VMEM((4, 3 * 256, 256), BF16),
+            pltpu.VMEM((2, 3 * LANE, LANE), BF16),
             pltpu.VMEM(wide, F32),
             pltpu.VMEM(wide, F32),
             pltpu.VMEM((2, LEVS, LON), F32),
             pltpu.VMEM((2, LEVS, LON), F32),
             pltpu.VMEM((5, ROWS * LEVS, LANE), F32),
+            pltpu.VMEM(full, F32),
+            pltpu.VMEM(full, F32),
             pltpu.VMEM(line, F32),
             pltpu.VMEM(line, F32),
             pltpu.VMEM(line, F32),
@@ -582,14 +717,15 @@
             pltpu.VMEM(line, F32),
             pltpu.VMEM((3,) + line, F32),
             pltpu.VMEM(line, F32),
-            pltpu.VMEM((2, 4, 2, ROWS * LEVS, 2 * LANE), BF16),
-            pltpu.VMEM((2, 2, ROWS * LEVS, LANE), BF16),
-            pltpu.VMEM((2, 4, ROWS * LEVS, 2 * LANE), F32),
-            pltpu.VMEM((2, ROWS * LEVS, LANE), F32),
-            dma((12,)), dma((6, 2)), dma((6, 2)), dma((2, 2)), dma((2, 2)),
+            pltpu.VMEM((4, 2 * ROWS * LEVS, 6 * LANE), BF16),
+            pltpu.VMEM((2 * ROWS * LEVS, 3 * LANE), BF16),
+            pltpu.VMEM((4, 2 * ROWS * LEVS, 2 * LANE), F32),
+            pltpu.VMEM((2 * ROWS * LEVS, LANE), F32),
+            pltpu.SemaphoreType.REGULAR, dma((12,)), dma((6, 2)), dma((6, 2)), dma((2, 2)), dma((2, 2)),
+            dma((NCHUNK, 2)), dma((NCHUNK, 2)),
         ]
         + scan_sems
-        + scan_sems,
+        + scan_sems[2:],
         compiler_params=pltpu.CompilerParams(
             collective_id=0, has_side_effects=True, vmem_limit_bytes=40 << 20
         ),

time: 43.3 us -> 36.5 us (0.84)
  the two profiles are of different devices: /device:TPU:1 before, /device:TPU:33 now
where the time goes in v1:
time: 36.5 us; the launch traced here: 36.3 us
  Pallas kernels  35.7 us (98%)
  between operations  0.64 us (2%)
    pallas_call x1, Pallas kernels, shards(): pl.pallas_call(first_kernel, out_shape=[pltpu.VMEM(wide, F32)] + [pltpu.V...  33 us
    pallas_call x1, Pallas kernels, shards(): pl.pallas_call(second_kernel, out_shape=[jax.ShapeDtypeStruct(full, F32)]...  2.73 us

profile of v1, /device:TPU:33, one launch (start us, length us, event | category | flops | bytes accessed | tf_op | source)
XLA Modules:
  0.0 36.3 jit_solution(14118644725568577441)
XLA Ops:
  0.6 33.0 %shard_map.171 = (f32[26,8,1152]{2,1,0:T(8,128)S(1)}, f32[24,8,1152]{2,1,0:T(8,128)S(1)}, f32[24,8,1152]{2,1,0:T(8,128)S(1)}, f32[24,8,1152]{2,1,0:T(8,128)S(1)}...) custom-call(f32[24,8,1152]{2,1,0:T(8,128)} %u_hbm.1, ...), custom_call_target="tpu_custom_call" | custom-call | tf_op jit(solution)/shard_map/pallas_call | solution.py:686
  33.6 2.7 %shard_map.172 = (f32[24,8,1152]{2,1,0:T(8,128)}, f32[24,8,1152]{2,1,0:T(8,128)}, f32[24,8,1152]{2,1,0:T(8,128)}, f32[24,8,1152]{2,1,0:T(8,128)}, f32[24,8,1152]...) custom-call(f32[26,8,1152]{2,1,0:T(8,128)S(1)} %get-tuple-element.15.height, ...), custom_call_target="tpu_custom_call" | custom-call | tf_op jit(solution)/shard_map/pallas_call | solution.py:733

commit v2 on v1

--- a/solution.py
+++ b/solution.py
@@ -75,10 +75,12 @@
     cum, logmid, halo_t, halo_p, damp, pair_t, pair_c,
     s_own, s_pair, s_chip, s_recv, pre, pre_pair,
     d_own, d_pair, d_chip, d_recv, geo_pair,
+    edge_s, edge_d, edge_h, both_chips,
     y4, y1, z4, z1,
     ready, load_sem, halo_s, halo_r, out_s, out_r, both_s, both_r,
     bp_s, bp_r, bz_s, bz_r, bq_s, bq_r, be_s, be_r,
     cz_s, cz_r, cq_s, cq_r, ce_s, ce_r,
+    ez_s, ez_r, dz_s, dz_r, hz_s, hz_r,
 ):
     la, le = lax.axis_index("lat"), lax.axis_index("lev")
     chip, core = le // 2, le % 2
@@ -114,8 +116,17 @@
     barrier = pltpu.get_barrier_semaphore()
     upper = chip < CHIPS // 2
     others = [(chip + d) % CHIPS for d in range(1, CHIPS)]
-    greet = [(la >= 0, pair_dev), (has_up, (up, le)), (has_down, (down, le)), (has_side, cross_dev)]
-    greet += [(upper | (c >= CHIPS // 2), (la, c * 2 + core)) for c in others]
+    starts, ends = la == NLAT // 2, la == NLAT // 2 - 1
+    to_up = [(has_up, (up, le)), (has_up & (core == 1), cross_dev)]
+    to_down = [(has_down, (down, le)), (has_down & (core == 0), cross_dev)]
+    far_up = [(has_up & (c > chip), (up, c * 2)) for c in others]
+    far_down = [(has_down & (c > chip), (down, c * 2 + 1)) for c in others]
+    n_up = has_up.astype(jnp.int32) + jnp.where(has_up & (core == 1), 1 + 2 * chip, 0)
+    n_down = has_down.astype(jnp.int32) + jnp.where(has_down & (core == 0), 1 + 2 * chip, 0)
+    greet = [(la >= 0, pair_dev)] + to_down + far_down + [(there & ~ends, dev) for there, dev in to_up + far_up]
+    for c in others:
+        inside = upper | (c >= CHIPS // 2)
+        greet += [(inside, (la, c * 2 + core)), (inside, (la, c * 2 + other))]
     for there, dev in greet:
 
         @pl.when(there)
@@ -134,24 +145,38 @@
             ins[f].at[0], fields.at[f, ROWS + 1], halo_s.at[f, 1], halo_r.at[f, 1], (down, le)
         )
 
-    seam = la == NLAT // 2 - 1
+    seam = starts | ends
+    hub = (starts & (core == 0)) | (ends & (core == 1))
 
     def halo_start(f):
-        pl.when(has_up & ~seam)(halo[f, 0].start)
-        pl.when(has_down)(halo[f, 1].start)
+        pl.when(has_up & ~ends)(halo[f, 0].start)
+        pl.when(has_down & ~starts)(halo[f, 1].start)
 
     def enter():
-        near = has_up.astype(jnp.int32) + has_down.astype(jnp.int32) + has_side.astype(jnp.int32)
-        pl.semaphore_wait(barrier, near + jnp.where(upper, 2, 4))
+        pl.semaphore_wait(barrier, jnp.where(upper, 3, 7) + n_up + jnp.where(starts, 0, n_down))
 
         @pl.when(~upper)
         def _():
-            for c in range(CHIPS // 2):
-                pl.semaphore_signal(ready, inc=1, device_id=(la, c * 2 + core), device_id_type=MESH)
+            for c in range(CHIPS):
+                at = ready.at[jnp.where(c // 2 == CHIPS - 1 - chip, 0, 1)]
+                pl.semaphore_signal(at, inc=1, device_id=(la, c), device_id_type=MESH)
+
+        for there, dev in to_up:
+
+            @pl.when(there & ends)
+            def _():
+                pl.semaphore_signal(ready.at[2], inc=1, device_id=dev, device_id_type=MESH)
 
         for f in (3, 2):
             pl.when(has_up)(halo[f, 0].start)
-            pl.when(has_down)(halo[f, 1].start)
+            pl.when(has_down & ~starts)(halo[f, 1].start)
+
+    def enter_down():
+        @pl.when(starts)
+        def _():
+            pl.semaphore_wait(ready.at[2], 2 - core)
+            for f in (3, 2):
+                halo[f, 1].start()
 
     enter()
 
@@ -176,22 +201,18 @@
         merid = fields[f, j + 2] - fields[f, j]
         return x - COURANT * (fields[0, j + 1] * east_west(x) + fields[1, j + 1] * merid)
 
+    def halo_side(f, side):
+        edge, there = (1, has_down) if side == 0 else (ROWS, has_up)
+        beyond = (ROWS + 1) * side
+        pl.when(there)(halo[f, side].wait_recv)
+
+        @pl.when(~there)
+        def _():
+            fields[f, beyond] = fields[f, edge]
+
     def halo_ready(f):
-        @pl.when(has_down)
-        def _():
-            halo[f, 0].wait_recv()
-
-        @pl.when(has_up)
-        def _():
-            halo[f, 1].wait_recv()
-
-        @pl.when(la == 0)
-        def _():
-            fields[f, 0] = fields[f, 1]
-
-        @pl.when(la == NLAT - 1)
-        def _():
-            fields[f, ROWS + 1] = fields[f, ROWS]
+        halo_side(f, 0)
+        halo_side(f, 1)
 
     def column_t(j):
         t_out[j] = advected(2, j)
@@ -233,7 +254,15 @@
             result_pair.at[theirs_s], result.at[pl.ds(theirs + 1, n)], qs.at[k], qr.at[k], pair_dev
         )
         hops = {}
-        for d in (2, 1, 3):
+        buddy = remote(
+            total.at[mine_s], recv.at[0, mine_s], zs.at[k, 0], zr.at[k, 0],
+            (la, (chip + 1 - 2 * (chip % 2)) * 2 + core),
+        )
+        relay = remote(
+            both_chips.at[mine_s], recv.at[1, mine_s], zs.at[k, 1], zr.at[k, 1],
+            (la, (CHIPS - 1 - chip) * 2 + core),
+        )
+        for d in (3, 2, 1):
             hops[d] = remote(
                 total.at[mine_s], recv.at[d - 1, mine_s], zs.at[k, d - 1], zr.at[k, d - 1],
                 (la, ((chip + CHIPS + sign * d) % CHIPS) * 2 + core),
@@ -246,6 +275,14 @@
             gets = {d: chip + d < CHIPS for d in hops}
         edges = []
         if k == EDGE:
+            direct = {
+                (d, w): remote(
+                    own.at[(ROWS - 1) * w], edge_s.at[d - 1, core], ez_s.at[d - 1, w], ez_r.at[d - 1, core],
+                    (la, ((chip + d) % CHIPS) * 2 + w),
+                )
+                for d in (1, 2, 3)
+                for w in range(2)
+            }
             slot = (ROWS + 1) * other
             edges = [
                 remote(result.at[mine + 1], result.at[slot], es.at[0], er.at[other], side_dev),
@@ -255,27 +292,57 @@
         def begin():
             to_pair.start()
 
-        def middle():
+        def middle(row=None):
+            if k == EDGE:
+                for (d, w), c in direct.items():
+                    if w == row:
+                        pl.when(sends[d])(c.start)
+                return
             if ps is not None:
                 from_pair.wait_recv()
             total[mine_s] = own[mine_s] + pair[mine_s]
             if sign > 0:
-                pl.when(chip % 2 == 0)(hops[1].start)
+                pl.when(chip < CHIPS - 1)(buddy.start)
             else:
                 for d in hops:
                     pl.when(sends[d])(hops[d].start)
 
         def across():
-            for d in hops:
-                pl.when(upper & sends[d] & ((chip + d) >= CHIPS // 2))(hops[d].start)
+            buddy.wait_recv()
+            both_chips[mine_s] = total[mine_s] + recv[0, mine_s]
+            relay.start()
 
         def end():
             acc = base(mine, n)
             result[pl.ds(mine + 1, n)] = acc
-            for d in hops:
+            if k == EDGE:
+                from_pair.wait_recv()
+            if sign > 0 and k != EDGE:
+
+                @pl.when(chip == CHIPS - 1)
+                def _():
+                    buddy.wait_recv()
+
+                @pl.when(chip % 2 == 1)
+                def _():
+                    result[pl.ds(mine + 1, n)] = result[pl.ds(mine + 1, n)] + recv[0, mine_s]
+
+                @pl.when(~upper)
+                def _():
+                    relay.wait_recv()
+                    result[pl.ds(mine + 1, n)] = result[pl.ds(mine + 1, n)] + recv[1, mine_s]
+
+            for d in hops if sign < 0 or k == EDGE else ():
 
                 @pl.when(gets[d])
                 def _():
+                    if k == EDGE:
+                        for w in range(2):
+                            remote(
+                                edge_s.at[d - 1, w], edge_s.at[d - 1, w], ez_s.at[d - 1, w], ez_r.at[d - 1, w], pair_dev
+                            ).wait_recv()
+                        result[mine + 1] = result[mine + 1] + (edge_s[d - 1, 0] + edge_s[d - 1, 1])
+                        return
                     hops[d].wait_recv()
                     result[pl.ds(mine + 1, n)] = result[pl.ds(mine + 1, n)] + recv[d - 1, mine_s]
 
@@ -300,8 +367,15 @@
             if ps is not None:
                 to_pair.wait_send()
             share.wait_send()
-            for d in hops:
-                pl.when(sends[d])(hops[d].wait_send)
+            if k == EDGE:
+                for (d, _), c in direct.items():
+                    pl.when(sends[d])(c.wait_send)
+            elif sign > 0:
+                pl.when(chip < CHIPS - 1)(buddy.wait_send)
+                pl.when(upper)(relay.wait_send)
+            else:
+                for d in hops:
+                    pl.when(sends[d])(hops[d].wait_send)
             for e in edges:
                 pl.when(has_side)(e.wait_send)
 
@@ -325,8 +399,86 @@
             k, d_own, d_pair, d_chip, d_recv, geo_off, geo_pair, -1, base_terrain,
             cz_s, cz_r, cq_s, cq_r, ce_s, ce_r,
         )
-        for k in range(NCHUNK)
+        for k in range(EDGE)
     ]
+
+    edge_row = (ROWS - 1) * core
+    edge_sends = []
+    for d in (3, 2, 1):
+        above = chip + CHIPS - d
+        for tc in range(2):
+            edge_sends.append((
+                has_side & (chip >= d),
+                remote(
+                    d_chip.at[edge_row], edge_h.at[other, d - 1], hz_s.at[d - 1, tc], hz_r.at[other, d - 1],
+                    (side_lat, (above % CHIPS) * 2 + tc),
+                ),
+            ))
+            edge_sends.append((
+                chip >= d,
+                remote(
+                    d_chip.at[edge_row], edge_d.at[core, d - 1], dz_s.at[d - 1, tc], dz_r.at[core, d - 1],
+                    (la, (above % CHIPS) * 2 + tc),
+                ),
+            ))
+    edge_slot = (ROWS + 1) * other
+    edge_sends += [
+        (has_side, remote(geo_pair.at[edge_row], geo_off.at[edge_slot], ce_s.at[0], ce_r.at[other], side_dev)),
+        (has_side, remote(geo_pair.at[(ROWS - 1) * other], geo_off.at[edge_slot], ce_s.at[1], ce_r.at[other], cross_dev)),
+    ]
+    last = ROWS - 1
+    to_upper = remote(d_own.at[last], d_pair.at[last], cq_s.at[EDGE], cq_r.at[EDGE], pair_dev)
+
+    def edge_depths():
+        own, pair = d_own[edge_row], d_pair[edge_row]
+        d_chip[edge_row] = own + pair
+        ground = terr[pl.ds(edge_row, 1), :]
+        geo_pair[0] = ground + jnp.where(core == 0, pair, own)
+        geo_pair[ROWS - 1] = ground
+        for there, c in edge_sends:
+            pl.when(there)(c.start)
+        pl.when(core == 1)(to_upper.start)
+
+    def edge_offsets():
+        for w in range(2):
+            r = last * w
+            geo_off[r + 1] = terr[pl.ds(r, 1), :]
+
+        @pl.when(core == 0)
+        def _():
+            to_upper.wait_recv()
+            for w in range(2):
+                geo_off[last * w + 1] = geo_off[last * w + 1] + d_pair[last * w]
+
+        for side, there in ((0, has_down), (1, has_up)):
+            slot = (ROWS + 1) * side
+
+            @pl.when(there)
+            def _():
+                remote(geo_off.at[slot], geo_off.at[slot], ce_s.at[0], ce_r.at[side], side_dev).wait_recv()
+
+        for d in (1, 2, 3):
+            for w in range(2):
+
+                @pl.when(chip + d < CHIPS)
+                def _():
+                    slot = edge_d.at[w, d - 1]
+                    remote(slot, slot, dz_s.at[0, 0], dz_r.at[w, d - 1], pair_dev).wait_recv()
+                    geo_off[last * w + 1] = geo_off[last * w + 1] + edge_d[w, d - 1]
+
+            for side, there in ((0, has_down), (1, has_up)):
+
+                @pl.when(there & (chip + d < CHIPS))
+                def _():
+                    slot = edge_h.at[side, d - 1]
+                    remote(slot, slot, dz_s.at[0, 0], hz_r.at[side, d - 1], pair_dev).wait_recv()
+                    i = (ROWS + 1) * side
+                    geo_off[i] = geo_off[i] + edge_h[side, d - 1]
+
+    def edge_drain():
+        for there, c in edge_sends:
+            pl.when(there)(c.wait_send)
+        pl.when(core == 1)(to_upper.wait_send)
 
     def thickness(i, temp):
         base = pre[i]
@@ -407,20 +559,10 @@
 
     @pl.when(upper)
     def _():
-        pl.semaphore_wait(ready, CHIPS // 2)
-
-    for k in range(EDGE):
-        top[k][6]()
-
-    halo_ready(3)
-    column_p(0)
-    column_p(ROWS - 1)
-    top[EDGE][0]()
-    halo_ready(2)
-    column_t(0)
-    column_t(ROWS - 1)
-    for c in pairs[EDGE]:
-        c.start()
+        pl.semaphore_wait(ready.at[0], 2)
+        for k in range(EDGE):
+            top[k][6]()
+
     out_copies = []
     for n, (src, dst) in enumerate(((t_out, halo_t), (p_out, halo_p))):
         out_copies.append(
@@ -428,19 +570,42 @@
         )
         out_copies.append(remote(src.at[0], dst.at[1], out_s.at[n, 1], out_r.at[n, 1], (down, le)))
     ways = (has_up, has_down)
-    top[EDGE][1]()
-    top[EDGE][6]()
-    for n, c in enumerate(out_copies):
-        pl.when(ways[n % 2])(c.start)
-
-    @pl.when(seam)
+
+    def edge_rows(w):
+        r = (ROWS - 1) * w
+        halo_side(3, w)
+        column_p(r)
+        pl.when(core != w)(top[EDGE][0])
+        top[EDGE][1](w)
+        halo_side(2, w)
+        column_t(r)
+        for c in pairs[EDGE]:
+            pl.when(core != w)(c.start)
+        for n, c in enumerate(out_copies):
+            if n % 2 != w:
+                pl.when(ways[n % 2])(c.start)
+
+    def edge_sums():
+        top[EDGE][2]()
+        for c in pairs[EDGE]:
+            c.wait_recv()
+        mine_rows(EDGE)
+        edge_depths()
+
+    def seam_rows():
+        pl.when(starts)(functools.partial(edge_rows, 0))
+        pl.when(ends)(functools.partial(edge_rows, 1))
+
+    enter_down()
+
+    @pl.when(upper)
     def _():
-        halo[0, 0].start()
-        halo[1, 0].start()
-
+        pl.semaphore_wait(ready.at[1], 2)
+
+    pl.when(~starts)(functools.partial(edge_rows, 0))
+    pl.when(~ends)(functools.partial(edge_rows, 1))
     for f in (4, 5):
-        pl.when(has_up)(halo[f, 0].start)
-        pl.when(has_down)(halo[f, 1].start)
+        halo_start(f)
 
     for n in (4, 5, 6, 7, 8, 9, 10, 11):
         load[n].wait()
@@ -531,7 +696,6 @@
     polar = (la < POLAR) | (la >= NLAT - POLAR)
 
     def forward():
-        prepare()
         halo_ready(0)
         halo_ready(1)
 
@@ -539,7 +703,8 @@
         def _(i):
             forward_nine(i)
 
-    pl.when(upper)(inner_tracers)
+    inner_tracers()
+    pl.when(polar)(prepare)
     pl.when(polar & upper)(forward)
 
     for k in range(EDGE):
@@ -548,15 +713,15 @@
             c.wait_recv()
         mine_rows(k)
         bottom[k][1]()
-    top[EDGE][2]()
-    for c in pairs[EDGE]:
-        c.wait_recv()
-    mine_rows(EDGE)
-    bottom[EDGE][1]()
+    pl.when(hub)(seam_rows)
+    edge_sums()
+    pl.when(seam & ~hub)(seam_rows)
+    for f in (0, 1, 4, 5):
+        pl.when(ends)(halo[f, 0].start)
+        pl.when(starts)(halo[f, 1].start)
     for k in range(NCHUNK):
         top[k][3]()
         their_rows(k)
-    pl.when(~upper)(inner_tracers)
     pl.when(polar & ~upper)(forward)
 
     @pl.when(polar)
@@ -614,11 +779,11 @@
     gradient_row(0)
     gradient_row(ROWS - 1)
 
-    for k in range(NCHUNK):
+    for k in range(EDGE):
         bottom[k][2]()
-    for k in range(NCHUNK):
+    edge_offsets()
+    for k in range(EDGE):
         bottom[k][3]()
-    bottom[EDGE][4]()
 
     @pl.when(la == 0)
     def _():
@@ -630,7 +795,9 @@
 
     for k in range(NCHUNK):
         top[k][5]()
+    for k in range(EDGE):
         bottom[k][5]()
+    edge_drain()
     for pair in pairs:
         for c in pair:
             c.wait_send()
@@ -717,15 +884,20 @@
             pltpu.VMEM(line, F32),
             pltpu.VMEM((3,) + line, F32),
             pltpu.VMEM(line, F32),
+            pltpu.VMEM((3, 2, 1, LON), F32),
+            pltpu.VMEM((2, 3, 1, LON), F32),
+            pltpu.VMEM((2, 3, 1, LON), F32),
+            pltpu.VMEM(line, F32),
             pltpu.VMEM((4, 2 * ROWS * LEVS, 6 * LANE), BF16),
             pltpu.VMEM((2 * ROWS * LEVS, 3 * LANE), BF16),
             pltpu.VMEM((4, 2 * ROWS * LEVS, 2 * LANE), F32),
             pltpu.VMEM((2 * ROWS * LEVS, LANE), F32),
-            pltpu.SemaphoreType.REGULAR, dma((12,)), dma((6, 2)), dma((6, 2)), dma((2, 2)), dma((2, 2)),
+            pltpu.SemaphoreType.REGULAR((3,)), dma((12,)), dma((6, 2)), dma((6, 2)), dma((2, 2)), dma((2, 2)),
             dma((NCHUNK, 2)), dma((NCHUNK, 2)),
         ]
         + scan_sems
-        + scan_sems[2:],
+        + scan_sems[2:]
+        + [dma((3, 2)), dma((3, 2)), dma((3, 2)), dma((2, 3)), dma((3, 2)), dma((2, 3))],
         compiler_params=pltpu.CompilerParams(
             collective_id=0, has_side_effects=True, vmem_limit_bytes=40 << 20
         ),

time: 36.5 us -> 34.7 us (0.951)
  Pallas kernels: 35.7 us -> 33.9 us
    pallas_call x1, Pallas kernels: 33 us -> 31.2 us  [shards(): pl.pallas_call(first_kernel, out_shape=[pltpu.VMEM(wide, F32)] + [pltpu.V...]
where the time goes in v2:
time: 34.7 us; the launch traced here: 34.6 us
  Pallas kernels  33.9 us (98%)
  between operations  0.64 us (2%)
    pallas_call x1, Pallas kernels, shards(): pl.pallas_call(first_kernel, out_shape=[pltpu.VMEM(wide, F32)] + [pltpu.V...  31.2 us
    pallas_call x1, Pallas kernels, shards(): pl.pallas_call(second_kernel, out_shape=[jax.ShapeDtypeStruct(full, F32)]...  2.73 us

profile of v2, /device:TPU:33, one launch (start us, length us, event | category | flops | bytes accessed | tf_op | source)
XLA Modules:
  0.0 34.6 jit_solution(12634406413351656781)
XLA Ops:
  0.6 31.2 %shard_map.171 = (f32[26,8,1152]{2,1,0:T(8,128)S(1)}, f32[24,8,1152]{2,1,0:T(8,128)S(1)}, f32[24,8,1152]{2,1,0:T(8,128)S(1)}, f32[24,8,1152]{2,1,0:T(8,128)S(1)}...) custom-call(f32[24,8,1152]{2,1,0:T(8,128)} %u_hbm.1, ...), custom_call_target="tpu_custom_call" | custom-call | tf_op jit(solution)/shard_map/pallas_call | solution.py:853
  31.8 2.7 %shard_map.172 = (f32[24,8,1152]{2,1,0:T(8,128)}, f32[24,8,1152]{2,1,0:T(8,128)}, f32[24,8,1152]{2,1,0:T(8,128)}, f32[24,8,1152]{2,1,0:T(8,128)}, f32[24,8,1152]...) custom-call(f32[26,8,1152]{2,1,0:T(8,128)S(1)} %get-tuple-element.15.height, ...), custom_call_target="tpu_custom_call" | custom-call | tf_op jit(solution)/shard_map/pallas_call | solution.py:905

commit v3 on v2

--- a/solution.py
+++ b/solution.py
@@ -123,7 +123,7 @@
     far_down = [(has_down & (c > chip), (down, c * 2 + 1)) for c in others]
     n_up = has_up.astype(jnp.int32) + jnp.where(has_up & (core == 1), 1 + 2 * chip, 0)
     n_down = has_down.astype(jnp.int32) + jnp.where(has_down & (core == 0), 1 + 2 * chip, 0)
-    greet = [(la >= 0, pair_dev)] + to_down + far_down + [(there & ~ends, dev) for there, dev in to_up + far_up]
+    greet = [(la >= 0, pair_dev)] + to_down + far_down + to_up + far_up
     for c in others:
         inside = upper | (c >= CHIPS // 2)
         greet += [(inside, (la, c * 2 + core)), (inside, (la, c * 2 + other))]
@@ -145,15 +145,13 @@
             ins[f].at[0], fields.at[f, ROWS + 1], halo_s.at[f, 1], halo_r.at[f, 1], (down, le)
         )
 
-    seam = starts | ends
-    hub = (starts & (core == 0)) | (ends & (core == 1))
 
     def halo_start(f):
         pl.when(has_up & ~ends)(halo[f, 0].start)
         pl.when(has_down & ~starts)(halo[f, 1].start)
 
     def enter():
-        pl.semaphore_wait(barrier, jnp.where(upper, 3, 7) + n_up + jnp.where(starts, 0, n_down))
+        pl.semaphore_wait(barrier, jnp.where(upper, 3, 7) + n_up + n_down)
 
         @pl.when(~upper)
         def _():
@@ -161,22 +159,9 @@
                 at = ready.at[jnp.where(c // 2 == CHIPS - 1 - chip, 0, 1)]
                 pl.semaphore_signal(at, inc=1, device_id=(la, c), device_id_type=MESH)
 
-        for there, dev in to_up:
-
-            @pl.when(there & ends)
-            def _():
-                pl.semaphore_signal(ready.at[2], inc=1, device_id=dev, device_id_type=MESH)
-
         for f in (3, 2):
             pl.when(has_up)(halo[f, 0].start)
-            pl.when(has_down & ~starts)(halo[f, 1].start)
-
-    def enter_down():
-        @pl.when(starts)
-        def _():
-            pl.semaphore_wait(ready.at[2], 2 - core)
-            for f in (3, 2):
-                halo[f, 1].start()
+            pl.when(has_down)(halo[f, 1].start)
 
     enter()
 
@@ -237,7 +222,7 @@
         else:
             start, n = INTERIOR[k]
 
-            @pl.loop(start, start + 2 * n, unroll=2)
+            @pl.loop(start, start + 2 * n, unroll=n)
             def _(j):
                 body(j)
 
@@ -535,7 +520,7 @@
         b_out[j] = advected(5, j)
 
     def inner_tracers():
-        @pl.loop(1, ROWS - 1, unroll=2)
+        @pl.loop(1, ROWS - 1, unroll=11)
         def _(j):
             tracers(j)
 
@@ -592,20 +577,18 @@
         mine_rows(EDGE)
         edge_depths()
 
-    def seam_rows():
-        pl.when(starts)(functools.partial(edge_rows, 0))
-        pl.when(ends)(functools.partial(edge_rows, 1))
-
-    enter_down()
-
     @pl.when(upper)
     def _():
         pl.semaphore_wait(ready.at[1], 2)
 
     pl.when(~starts)(functools.partial(edge_rows, 0))
-    pl.when(~ends)(functools.partial(edge_rows, 1))
+    edge_rows(1)
+    pl.when(starts)(functools.partial(edge_rows, 0))
     for f in (4, 5):
         halo_start(f)
+    for f in (0, 1):
+        pl.when(ends)(halo[f, 0].start)
+        pl.when(starts)(halo[f, 1].start)
 
     for n in (4, 5, 6, 7, 8, 9, 10, 11):
         load[n].wait()
@@ -703,9 +686,15 @@
         def _(i):
             forward_nine(i)
 
-    inner_tracers()
-    pl.when(polar)(prepare)
-    pl.when(polar & upper)(forward)
+    def early_fill():
+        inner_tracers()
+
+        @pl.when(polar)
+        def _():
+            prepare()
+            forward()
+
+    pl.when(upper)(early_fill)
 
     for k in range(EDGE):
         top[k][2]()
@@ -713,16 +702,14 @@
             c.wait_recv()
         mine_rows(k)
         bottom[k][1]()
-    pl.when(hub)(seam_rows)
     edge_sums()
-    pl.when(seam & ~hub)(seam_rows)
-    for f in (0, 1, 4, 5):
+    for f in (4, 5):
         pl.when(ends)(halo[f, 0].start)
         pl.when(starts)(halo[f, 1].start)
     for k in range(NCHUNK):
         top[k][3]()
         their_rows(k)
-    pl.when(polar & ~upper)(forward)
+    pl.when(~upper)(early_fill)
 
     @pl.when(polar)
     def _():
@@ -735,7 +722,7 @@
 
     @pl.when(~polar)
     def _():
-        @pl.loop(1, ROWS - 1, unroll=2)
+        @pl.loop(1, ROWS - 1, unroll=11)
         def _(j):
             east[j] = advected(0, j)
             north[j] = advected(1, j)
@@ -746,7 +733,7 @@
             east[j] = advected(0, j)
             north[j] = advected(1, j)
 
-    @pl.loop(1, ROWS - 1, unroll=2)
+    @pl.loop(1, ROWS - 1, unroll=11)
     def _(j):
         gradient_row(j)
 
@@ -892,7 +879,7 @@
             pltpu.VMEM((2 * ROWS * LEVS, 3 * LANE), BF16),
             pltpu.VMEM((4, 2 * ROWS * LEVS, 2 * LANE), F32),
             pltpu.VMEM((2 * ROWS * LEVS, LANE), F32),
-            pltpu.SemaphoreType.REGULAR((3,)), dma((12,)), dma((6, 2)), dma((6, 2)), dma((2, 2)), dma((2, 2)),
+            pltpu.SemaphoreType.REGULAR((2,)), dma((12,)), dma((6, 2)), dma((6, 2)), dma((2, 2)), dma((2, 2)),
             dma((NCHUNK, 2)), dma((NCHUNK, 2)),
         ]
         + scan_sems

time: 34.7 us -> 31.5 us (0.908)
  the two profiles are of different devices: /device:TPU:33 before, /device:TPU:225 now
where the time goes in v3:
time: 31.5 us; the launch traced here: 31.4 us
  Pallas kernels  30.8 us (98%)
  between operations  0.64 us (2%)
    pallas_call x1, Pallas kernels, shards(): pl.pallas_call(first_kernel, out_shape=[pltpu.VMEM(wide, F32)] + [pltpu.V...  28 us
    pallas_call x1, Pallas kernels, shards(): pl.pallas_call(second_kernel, out_shape=[jax.ShapeDtypeStruct(full, F32)]...  2.73 us

profile of v3, /device:TPU:225, one launch (start us, length us, event | category | flops | bytes accessed | tf_op | source)
XLA Modules:
  0.0 31.4 jit_solution(17906834375350356424)
XLA Ops:
  0.6 28.0 %shard_map.171 = (f32[26,8,1152]{2,1,0:T(8,128)S(1)}, f32[24,8,1152]{2,1,0:T(8,128)S(1)}, f32[24,8,1152]{2,1,0:T(8,128)S(1)}, f32[24,8,1152]{2,1,0:T(8,128)S(1)}...) custom-call(f32[24,8,1152]{2,1,0:T(8,128)} %u_hbm.1, ...), custom_call_target="tpu_custom_call" | custom-call | tf_op jit(solution)/shard_map/pallas_call | solution.py:840
  28.7 2.7 %shard_map.172 = (f32[24,8,1152]{2,1,0:T(8,128)}, f32[24,8,1152]{2,1,0:T(8,128)}, f32[24,8,1152]{2,1,0:T(8,128)}, f32[24,8,1152]{2,1,0:T(8,128)}, f32[24,8,1152]...) custom-call(f32[26,8,1152]{2,1,0:T(8,128)S(1)} %get-tuple-element.15.height, ...), custom_call_target="tpu_custom_call" | custom-call | tf_op jit(solution)/shard_map/pallas_call | solution.py:892

commit v4 on v3

--- a/solution.py
+++ b/solution.py
@@ -163,7 +163,7 @@
             pl.when(has_up)(halo[f, 0].start)
             pl.when(has_down)(halo[f, 1].start)
 
-    enter()
+    pl.when(~starts)(enter)
 
     row = lax.broadcasted_iota(jnp.int32, (LEVS, LON), 0)
 
@@ -351,7 +351,6 @@
         def drain():
             if ps is not None:
                 to_pair.wait_send()
-            share.wait_send()
             if k == EDGE:
                 for (d, _), c in direct.items():
                     pl.when(sends[d])(c.wait_send)
@@ -364,7 +363,10 @@
             for e in edges:
                 pl.when(has_side)(e.wait_send)
 
-        return begin, middle, end, finish, edge_ready, drain, across
+        def drain_share():
+            share.wait_send()
+
+        return begin, middle, end, finish, edge_ready, drain, across, drain_share
 
     def base_top(mine, n):
         return jnp.full((n, 1, LON), TOP, F32)
@@ -530,7 +532,14 @@
         load[f].start()
     for k in range(EDGE):
         chunk_rows(k, column_p)
-        top[k][0]()
+        pl.when(~starts)(top[k][0])
+
+    @pl.when(starts)
+    def _():
+        enter()
+        for k in range(EDGE):
+            top[k][0]()
+
     load[2].wait()
     pairs = [both(k) for k in range(NCHUNK)]
     for k in range(EDGE):
@@ -582,7 +591,7 @@
         pl.semaphore_wait(ready.at[1], 2)
 
     pl.when(~starts)(functools.partial(edge_rows, 0))
-    edge_rows(1)
+    pl.when(~(ends & ~upper))(functools.partial(edge_rows, 1))
     pl.when(starts)(functools.partial(edge_rows, 0))
     for f in (4, 5):
         halo_start(f)
@@ -702,6 +711,7 @@
             c.wait_recv()
         mine_rows(k)
         bottom[k][1]()
+    pl.when(ends & ~upper)(functools.partial(edge_rows, 1))
     edge_sums()
     for f in (4, 5):
         pl.when(ends)(halo[f, 0].start)
@@ -766,22 +776,9 @@
     gradient_row(0)
     gradient_row(ROWS - 1)
 
-    for k in range(EDGE):
-        bottom[k][2]()
-    edge_offsets()
-    for k in range(EDGE):
-        bottom[k][3]()
-
-    @pl.when(la == 0)
-    def _():
-        geo_off[0] = geo_off[1]
-
-    @pl.when(la == NLAT - 1)
-    def _():
-        geo_off[ROWS + 1] = geo_off[ROWS]
-
     for k in range(NCHUNK):
         top[k][5]()
+        top[k][7]()
     for k in range(EDGE):
         bottom[k][5]()
     edge_drain()
@@ -792,6 +789,21 @@
         pl.when(ways[side])(c.wait_send)
     for n, c in enumerate(out_copies):
         pl.when(ways[n % 2])(c.wait_send)
+    for k in range(EDGE):
+        bottom[k][2]()
+    edge_offsets()
+    for k in range(EDGE):
+        bottom[k][3]()
+
+    @pl.when(la == 0)
+    def _():
+        geo_off[0] = geo_off[1]
+
+    @pl.when(la == NLAT - 1)
+    def _():
+        geo_off[ROWS + 1] = geo_off[ROWS]
+    for k in range(EDGE):
+        bottom[k][7]()
 
 
 def second_kernel(

time: 31.5 us -> 30.5 us (0.968)
  the two profiles are of different devices: /device:TPU:225 before, /device:TPU:33 now
where the time goes in v4:
time: 30.5 us; the launch traced here: 30.4 us
  Pallas kernels  29.7 us (97%)
  between operations  0.64 us (2%)
    pallas_call x1, Pallas kernels, shards(): pl.pallas_call(first_kernel, out_shape=[pltpu.VMEM(wide, F32)] + [pltpu.V...  27 us
    pallas_call x1, Pallas kernels, shards(): pl.pallas_call(second_kernel, out_shape=[jax.ShapeDtypeStruct(full, F32)]...  2.73 us

profile of v4, /device:TPU:33, one launch (start us, length us, event | category | flops | bytes accessed | tf_op | source)
XLA Modules:
  0.0 30.4 jit_solution(1481544912956055784)
XLA Ops:
  0.6 27.0 %shard_map.171 = (f32[26,8,1152]{2,1,0:T(8,128)S(1)}, f32[24,8,1152]{2,1,0:T(8,128)S(1)}, f32[24,8,1152]{2,1,0:T(8,128)S(1)}, f32[24,8,1152]{2,1,0:T(8,128)S(1)}...) custom-call(f32[24,8,1152]{2,1,0:T(8,128)} %u_hbm.1, ...), custom_call_target="tpu_custom_call" | custom-call | tf_op jit(solution)/shard_map/pallas_call | solution.py:852
  27.6 2.7 %shard_map.172 = (f32[24,8,1152]{2,1,0:T(8,128)}, f32[24,8,1152]{2,1,0:T(8,128)}, f32[24,8,1152]{2,1,0:T(8,128)}, f32[24,8,1152]{2,1,0:T(8,128)}, f32[24,8,1152]...) custom-call(f32[26,8,1152]{2,1,0:T(8,128)S(1)} %get-tuple-element.15.height, ...), custom_call_target="tpu_custom_call" | custom-call | tf_op jit(solution)/shard_map/pallas_call | solution.py:904

commit v5 on v4

--- a/solution.py
+++ b/solution.py
@@ -592,12 +592,13 @@
 
     pl.when(~starts)(functools.partial(edge_rows, 0))
     pl.when(~(ends & ~upper))(functools.partial(edge_rows, 1))
-    pl.when(starts)(functools.partial(edge_rows, 0))
+    pl.when(starts & upper)(functools.partial(edge_rows, 0))
     for f in (4, 5):
         halo_start(f)
-    for f in (0, 1):
-        pl.when(ends)(halo[f, 0].start)
-        pl.when(starts)(halo[f, 1].start)
+    for f in (0, 1, 4, 5):
+        now = upper | (f < 2)
+        pl.when(ends & now)(halo[f, 0].start)
+        pl.when(starts & now)(halo[f, 1].start)
 
     for n in (4, 5, 6, 7, 8, 9, 10, 11):
         load[n].wait()
@@ -711,11 +712,12 @@
             c.wait_recv()
         mine_rows(k)
         bottom[k][1]()
+    pl.when(starts & ~upper)(functools.partial(edge_rows, 0))
     pl.when(ends & ~upper)(functools.partial(edge_rows, 1))
     edge_sums()
     for f in (4, 5):
-        pl.when(ends)(halo[f, 0].start)
-        pl.when(starts)(halo[f, 1].start)
+        pl.when(ends & ~upper)(halo[f, 0].start)
+        pl.when(starts & ~upper)(halo[f, 1].start)
     for k in range(NCHUNK):
         top[k][3]()
         their_rows(k)

time: 30.5 us -> 30.6 us (level)
  no operation moved by 1% of the time
where the time goes in v5:
time: 30.6 us; the launch traced here: 30.4 us
  Pallas kernels  29.8 us (97%)
  between operations  0.64 us (2%)
    pallas_call x1, Pallas kernels, shards(): pl.pallas_call(first_kernel, out_shape=[pltpu.VMEM(wide, F32)] + [pltpu.V...  27.1 us
    pallas_call x1, Pallas kernels, shards(): pl.pallas_call(second_kernel, out_shape=[jax.ShapeDtypeStruct(full, F32)]...  2.73 us

profile of v5, /device:TPU:33, one launch (start us, length us, event | category | flops | bytes accessed | tf_op | source)
XLA Modules:
  0.0 30.4 jit_solution(17739958428445949146)
XLA Ops:
  0.6 27.1 %shard_map.171 = (f32[26,8,1152]{2,1,0:T(8,128)S(1)}, f32[24,8,1152]{2,1,0:T(8,128)S(1)}, f32[24,8,1152]{2,1,0:T(8,128)S(1)}, f32[24,8,1152]{2,1,0:T(8,128)S(1)}...) custom-call(f32[24,8,1152]{2,1,0:T(8,128)} %u_hbm.1, ...), custom_call_target="tpu_custom_call" | custom-call | tf_op jit(solution)/shard_map/pallas_call | solution.py:854
  27.7 2.7 %shard_map.172 = (f32[24,8,1152]{2,1,0:T(8,128)}, f32[24,8,1152]{2,1,0:T(8,128)}, f32[24,8,1152]{2,1,0:T(8,128)}, f32[24,8,1152]{2,1,0:T(8,128)}, f32[24,8,1152]...) custom-call(f32[26,8,1152]{2,1,0:T(8,128)S(1)} %get-tuple-element.15.height, ...), custom_call_target="tpu_custom_call" | custom-call | tf_op jit(solution)/shard_map/pallas_call | solution.py:906
